TPU v7x, 32 devices: a whole 2x2x4 slice. The times are simulated.
32 devices in a mesh: sec: 8 (over y, x, core), dev: 4 (over z).
Axes of the slice: x: 2, y: 2, z: 4, core: 2. Of those that a mesh axis runs over, the one named last changes fastest.
Arguments:
- rhs_interior: bfloat16 [327680, 256], P(('sec', 'dev')), may hold values from -6 to 6
- rhs_interface: float32 [10240, 256], P(('sec', 'dev')), may hold values from -6 to 6
- inv_blocks: bfloat16 [1280, 256, 256], P(('sec', 'dev')), may hold values from -0.375 to 0.375
- coupling: bfloat16 [1280, 2, 64, 256], P(('sec', 'dev')), may hold values from -0.1875 to 0.1875
- interface_map: int32 [1280, 64], P(('sec', 'dev')), may hold values from 0 to 10239, as said below
- slot_counts: int32 [1280], P(('sec', 'dev')), may hold values from 32 to 64, as said below
- column_order: int32 [256], replicated, may hold values from 0 to 255, each once
- schur_inverse: bfloat16 [10240, 10240], P('dev', 'sec'), may hold values from -0.0625 to 0.0625
Outputs:
- interior_solution: bfloat16 [327680, 256], P(('sec', 'dev'))
- interface_solution: float32 [10240, 256], P('dev')
Inputs may be any that keep to these rules, and one draw needn't show every extreme that they name: `slot_counts`: every block has at least half of its 64 slots live, and some block has all 64 live. `interface_map`: split the interface rows into 32 equal ranges, range d belonging to the device of flat index d over sec+dev; of the 2560 slots of one device's blocks at most 160 point into any one range, the slots into ranges 2p and 2p + 1 together number exactly 160, and one range receives exactly 160 slots from every device.
All inputs are finite; a program needn't handle non-finite values.
Results may differ from a plain program's by a relative error of at most 0.0056.
Values may be sent and summed in bfloat16 or wider, within the bound.
A program may use at most 128 MiB of HBM per device.

v0:
```python
import jax
import jax.numpy as jnp
from jax import lax
from jax.sharding import PartitionSpec as P


def shards(
    rhs_interior,
    rhs_interface,
    inv_blocks,
    coupling,
    interface_map,
    slot_counts,
    column_order,
    schur_inverse,
):
    block_count = inv_blocks.shape[0]
    block_size = inv_blocks.shape[1]
    slot_count = coupling.shape[2]
    column_count = rhs_interior.shape[1]
    sec_size = lax.axis_size("sec")
    dev_size = lax.axis_size("dev")
    interface_rows = schur_inverse.shape[0] * dev_size
    piece_rows = interface_rows // (sec_size * dev_size)
    sec_index = lax.axis_index("sec")
    dev_index = lax.axis_index("dev")
    live_mask = jnp.arange(slot_count, dtype=jnp.int32)[None, :] < slot_counts[:, None]
    local_rhs = rhs_interior.reshape(block_count, block_size, column_count)
    solved = jnp.einsum(
        "bij,bjn->bin", inv_blocks, local_rhs, preferred_element_type=jnp.float32
    ).astype(jnp.bfloat16)
    solved = lax.optimization_barrier(solved)
    partials = jnp.einsum(
        "bkr,brn->bkn", coupling[:, 0], solved, preferred_element_type=jnp.float32
    )
    partials = jnp.where(live_mask[:, :, None], partials, 0.0).reshape(
        block_count * slot_count, column_count
    )
    rhs_cols = jnp.take(rhs_interface, column_order, axis=1)
    targets = interface_map.reshape(-1)
    own_first = (sec_index * dev_size + dev_index) * piece_rows
    dense_sums = jnp.zeros((interface_rows, column_count), jnp.float32).at[targets].add(-partials)
    own_rows = lax.dynamic_slice_in_dim(dense_sums, own_first, piece_rows, 0) + rhs_cols
    dense_sums = lax.dynamic_update_slice_in_dim(dense_sums, own_rows, own_first, 0)
    section_part = lax.psum_scatter(dense_sums, "sec", scatter_dimension=0, tiled=True)
    reduced = lax.psum(section_part, "dev")
    schur_part = jnp.dot(
        schur_inverse, reduced.astype(jnp.bfloat16), preferred_element_type=jnp.float32
    )
    interface_solution = lax.psum(schur_part, "sec")
    values = lax.all_gather(interface_solution.astype(jnp.bfloat16), "dev", axis=0, tiled=True)
    picked = jnp.take(values, interface_map.reshape(-1), axis=0).reshape(
        block_count, slot_count, column_count
    )
    picked = jnp.where(live_mask[:, :, None], picked, jnp.zeros((), jnp.bfloat16))
    pushed = jnp.einsum(
        "bkr,bkn->brn", coupling[:, 1], picked, preferred_element_type=jnp.float32
    ).astype(jnp.bfloat16)
    back_term = jnp.einsum("bij,bjn->bin", inv_blocks, pushed, preferred_element_type=jnp.float32)
    interior = (solved.astype(jnp.float32) - back_term).astype(jnp.bfloat16)
    return (interior.reshape(block_count * block_size, column_count), interface_solution)


def solution(mesh):
    placed = (
        P(("sec", "dev"), None),
        P(("sec", "dev"), None),
        P(("sec", "dev"), None, None),
        P(("sec", "dev"), None, None, None),
        P(("sec", "dev"), None),
        P(("sec", "dev")),
        P(),
        P("dev", "sec"),
    )
    return jax.shard_map(
        shards,
        mesh=mesh,
        in_specs=placed,
        out_specs=(P(("sec", "dev"), None), P("dev", None)),
        check_vma=False,
    )
```

profile of v0, /device:TPU:25, one launch (start us, length us, event | category | flops | bytes accessed | tf_op | source)
XLA Modules:
  0.0 379.1 jit_solution(6556808980414093241)
XLA Ops:
  7.2 0.0 reduce-scatter.2.cloned.1.call-start
  7.2 0.7 compare_and_fusion.1
  7.9 0.7 compare_select_fusion.2
  8.6 0.8 reshape.83
  9.4 0.8 iota_compare_fusion
  10.3 1.1 copy.16
  11.4 1.0 gather_fusion
  12.4 0.1 copy.17
  12.6 8.0 %convolution_convert_fusion = bf16[40,256,256]{2,1,0:T(8,128)(2,1)} fusion(bf16[40,256,256]{2,1,0:T(8,128)(2,1)} %param.10, bf16[40,256,256]{2,1,0:T(8,128)(2,1)} %bitcast.31), kind=kOutput, calls=%fused_computation.11 | convolution fusion | flops 1344798720 | bytes 15728640 | tf_op jit(solution)/shard_map/bij,bjn->bin/dot_general | solution.py:29
  20.5 3.8 %select_negate_fusion = f32[40,256,64]{1,2,0:T(8,128)S(1)} fusion(bf16[40,256,256]{2,1,0:T(8,128)(2,1)} %convolution_convert_fusion, bf16[40,2,64,256]{3,2,1,0:T(8,128)(2,1)} %param.11, pred[40,64]{1,0:T(8,128)(4,1)S(1)} %get-tuple-element.6), kind=kOutput, calls=%fused_computation.12 | convolution fusion | flops 336855040 | bytes 9177600 | tf_op jit(solution)/shard_map/bkr,brn->bkn/dot_general | solution.py:33
  24.4 18.9 %scatter_custom_fusion = f32[10240,256]{1,0:T(8,128)} fusion(s32[2560]{0:T(1024)S(1)} %fusion.29, f32[2560,256]{1,0:T(8,128)S(1)} %bitcast.32, f32[]{:T(128)} %constant.24.clone.1), kind=kCustom, calls=%fused_computation.7 | custom fusion | flops 655360 | bytes 10485764 | tf_op jit(solution)/shard_map/scatter-add | solution.py:42
  43.3 1.7 fusion.28
  45.0 0.0 all-reduce.3.cloned.1.call-start
  45.1 82.7 %reduce-scatter.2.cloned.1.call-done = f32[1280,256]{1,0:T(8,128)} async-done(((f32[10240,256]{1,0:T(8,128)}), f32[1280,256]{1,0:T(8,128)}) %reduce-scatter.2.cloned.1.call-update) | async-done | bytes 1310736 | tf_op jit(solution)/shard_map/reduce_scatter | solution.py:45
  127.8 47.6 %all-reduce.4 = bf16[1280,256]{1,0:T(8,128)(2,1)S(1)} all-reduce(f32[1280,256]{1,0:T(8,128)} %reduce-scatter.2.cloned.1.call-done), channel_id=1, replica_groups=mesh['sec'=8,'dev'=4] {'dev'}, use_global_device_ids=true, to_apply=%region_2.3 | all-reduce | flops 327680 | bytes 1966080 | tf_op jit(solution)/shard_map/psum | solution.py:46
  175.4 6.3 %convolution_bitcast_fusion = f32[2560,256]{0,1:T(8,128)} fusion(bf16[2560,1280]{1,0:T(8,128)(2,1)} %param.15, bf16[1280,256]{1,0:T(8,128)(2,1)S(1)} %all-reduce.4), kind=kOutput, calls=%fused_computation.9 | convolution fusion | flops 1677721600 | bytes 9830400 | tf_op jit(solution)/shard_map/dot_general | solution.py:47
  181.7 0.2 all-gather.2.cloned.1.call-start
  181.9 66.7 %all-reduce.3.cloned.1.call-done = f32[2560,256]{0,1:T(8,128)} async-done(((f32[2560,256]{0,1:T(8,128)}), f32[2560,256]{0,1:T(8,128)}) %all-reduce.3.cloned.1.call-update) | async-done | bytes 2621456 | tf_op jit(solution)/shard_map/psum | solution.py:50
  248.6 3.2 convert_element_type.22
  251.8 2.1 copy.19
  253.9 93.4 %all-gather.2.cloned.1.call-done = bf16[10240,256]{0,1:T(8,128)(2,1)} async-done(((bf16[2560,256]{0,1:T(8,128)(2,1)}), bf16[10240,256]{0,1:T(8,128)(2,1)}) %all-gather.2.cloned.1.call-update) | async-done | bytes 5242896 | tf_op jit(solution)/shard_map/all_gather | solution.py:51
  347.3 7.9 %copy.18 = bf16[10240,256]{1,0:T(8,128)(2,1)} copy(bf16[10240,256]{0,1:T(8,128)(2,1)} %all-gather.2.cloned.1.call-done) | data formatting | bytes 10485760 | tf_op jit(solution)/shard_map/all_gather | solution.py:51
  355.2 8.9 %gather_fusion.1 = bf16[2560,256]{1,0:T(8,128)(2,1)S(1)} fusion(bf16[10240,256]{1,0:T(8,128)(2,1)} %copy.18, s32[3072]{0:T(1024)S(1)} %pad_clamp_fusion), kind=kCustom, calls=%fused_computation.1 | custom fusion | bytes 2631680 | tf_op jit(solution)/shard_map/jit(_take)/gather | solution.py:52
  364.1 8.4 %fusion = bf16[40,256,256]{2,1,0:T(8,128)(2,1)} fusion(bf16[40,256,256]{2,1,0:T(8,128)(2,1)} %convolution_convert_fusion, bf16[40,256,256]{2,1,0:T(8,128)(2,1)} %param.10, bf16[40,2,64,256]{3,2,1,0:T(8,128)(2,1)} %param.11, bf16[40,64,256]{2,1,0:T(8,128)(2,1)S(1)} %bitcast.33, pred[40,64]{1,0:T(8,128)(4,1)S(1)} %get-tuple-element.7, ...), kind=kOutput, calls=%fused_computation.4 | convolution fusion | flops 1689518080 | bytes 18355200 | tf_op jit(solution)/shard_map/bij,bjn->bin/dot_general | solution.py:59
  (8 shorter events, 0.1 us)
Async XLA Ops:
  7.2 120.6 %reduce-scatter.2.cloned.1.call-start = ((), (), s32[]{:S(2)}) async-start(), calls=%async_computation.1 | async-start | bytes 11796480 | tf_op jit(solution)/shard_map/reduce_scatter | solution.py:45
  45.0 203.6 %all-reduce.3.cloned.1.call-start = ((), (), s32[]{:S(2)}) async-start(), calls=%async_computation.2 | async-start | bytes 5242880 | tf_op jit(solution)/shard_map/psum | solution.py:50
  181.7 165.6 %all-gather.2.cloned.1.call-start = ((), (), s32[]{:S(2)}) async-start(), calls=%async_computation.3 | async-start | bytes 6553600 | tf_op jit(solution)/shard_map/all_gather | solution.py:51
  248.6 3.2 copy-start
Sparse Core Ops, SparseCore 0:
  45.1 82.5 reduce-scatter.1
  181.8 66.7 all-reduce.2
  251.9 95.3 all-gather.1
where the time goes:
time: 384 us; the launch traced here: 379 us
  waiting for transfers between devices  243 us (63%)
  blocking collectives  47.6 us (12%)
  matrix products  26.5 us (7%)
  other arithmetic  26.1 us (7%)
  local copies, waits for them, and re-layouts  22 us (6%)
  between operations  13.8 us (4%)
    all_gather x1, waiting for transfers between devices, shards(): lax.all_gather(interface_solution.astype(jnp.bfloat16), 'dev', axis=0, ti...  93.4 us
    reduce_scatter x1, waiting for transfers between devices, shards(): lax.psum_scatter(dense_sums, 'sec', scatter_dimension=0, tiled=True)  82.7 us
    psum x1, waiting for transfers between devices, shards(): interface_solution = lax.psum(schur_part, 'sec')  66.7 us
    psum x1, blocking collectives, shards(): reduced = lax.psum(section_part, 'dev')  47.6 us
    scatter-add x1, other arithmetic, shards(): jnp.zeros((interface_rows, column_count), jnp.float32).at[targets]  18.9 us
    gather x1, local copies, waits for them, and re-layouts, shards(): jnp.take(values, interface_map.reshape(-1), axis=0)  8.89 us
    dot_general x1, matrix products, shards(): jnp.einsum('bij,bjn->bin', inv_blocks, pushed, preferred_element_type=jnp...  8.45 us
    dot_general x1, matrix products, shards(): jnp.einsum('bij,bjn->bin', inv_blocks, local_rhs, preferred_element_type=...  7.95 us
  transfers between devices with their start and end apart: 3, of which 3 were waited for; matrix products, arithmetic and copies ran while one was open for 1% of the time, Pallas kernels for 0%

commit v1 on v0

v1 whole, which is shorter than its diff:
```python
import functools
import math

import jax
import jax.numpy as jnp
from jax import lax
from jax.experimental import pallas as pl
from jax.experimental.pallas import tpu as pltpu
from jax.sharding import PartitionSpec as P

MESH = pl.DeviceIdType.MESH
F32 = jnp.float32
BF16 = jnp.bfloat16
VMEM_LIMIT = 56 * 1024 * 1024


def sort_kernel(place_ref, local_ref, rows_ref, sorted_ref, ids_ref):
    count, total = sorted_ref.shape[0], place_ref.shape[1]
    wanted = lax.broadcasted_iota(jnp.int32, (count, total), 0) + pl.program_id(0) * count
    hot = jnp.where(place_ref[...] == wanted, 1.0, 0.0).astype(BF16)
    sorted_ref[...] = jnp.dot(hot, rows_ref[...], preferred_element_type=F32).astype(BF16)
    ids_ref[...] = lax.dot_general(
        local_ref[...], hot, (((1,), (1,)), ((), ())), preferred_element_type=F32
    )[None]


def interface_kernel(
    S, D, C, PR, G,
    send_ref, ids_ref, rhs_ref, schur_ref,
    values_ref, picked_ref,
    recv, ids_recv, acc, zsend, zrecv, red, psend, precv, band, zval, gsend, picked,
    s_a, r_a, s_i, r_i, s_z, r_z, s_g, r_g, s_p, r_p, s_v, r_v, s_w, r_w, s_f, r_f, s_k, r_k, s_o,
):
    me_s, me_d = lax.axis_index("sec"), lax.axis_index("dev")
    half = PR // 2
    GC, GP = G * C, G * PR
    parity = lax.rem(me_s, 2)
    mate = me_s + 1 - 2 * parity
    quarter = me_s // 2

    def at_sec(i):
        return lax.rem(me_s + i, S)

    def at_dev(i):
        return lax.rem(me_d + i, D)

    def copy(src, dst, send, recv_sem, sec, dev):
        return pltpu.make_async_remote_copy(
            src_ref=src, dst_ref=dst, send_sem=send, recv_sem=recv_sem,
            device_id=(sec, dev), device_id_type=MESH,
        )

    barrier = pltpu.get_barrier_semaphore()
    for i in range(1, S):
        pl.semaphore_signal(barrier, inc=1, device_id=(at_sec(i), me_d), device_id_type=MESH)
    for i in range(1, D):
        pl.semaphore_signal(barrier, inc=1, device_id=(me_s, at_dev(i)), device_id_type=MESH)
    pl.semaphore_wait(barrier, S + D - 2)

    def ids_copy(i):
        return copy(ids_ref.at[at_sec(i)], ids_recv.at[i], s_i.at[i], r_i.at[i], at_sec(i), me_d)

    def a_copy(i):
        return copy(send_ref.at[at_sec(i)], recv.at[i], s_a.at[i], r_a.at[i], at_sec(i), me_d)

    def z_copy(i):
        return copy(zsend.at[i], zrecv.at[i], s_z.at[i], r_z.at[i], me_s, at_dev(i))

    def g_copy(i):
        return copy(red.at[me_d], red.at[me_d], s_g.at[i], r_g.at[i], me_s, at_dev(i))

    def p_copy(i):
        return copy(psend.at[i], precv.at[i], s_p.at[i], r_p.at[i], at_sec(i), me_d)

    def v_copy(i):
        return copy(band.at[me_s], band.at[me_s], s_v.at[i], r_v.at[i], at_sec(i), me_d)

    def w_copy(i):
        return copy(band.at[me_s], zval.at[me_d, parity], s_w.at[i], r_w.at[i], me_s, at_dev(i))

    def f_copy(i):
        from_dev = lax.rem(me_d - i + D, D)
        src = band.at[me_s] if i == 0 else zval.at[from_dev, parity]
        return copy(src, zval.at[from_dev, parity], s_f.at[i], r_f.at[i], mate, me_d)

    def k_copy(t):
        return copy(gsend.at[t], picked.at[quarter], s_k.at[t], r_k.at[t], at_sec(2 * t), me_d)

    for i in range(1, S):
        ids_copy(i).start()
        a_copy(i).start()

    def add_slots(rows, ids, first):
        for g in range(D // 2 // G):
            hot = jnp.where(
                lax.broadcasted_iota(jnp.int32, (GP, GC), 0) == ids[g : g + 1, :GC], 1.0, 0.0
            ).astype(BF16)
            part = jnp.dot(hot, rows[g * GC : (g + 1) * GC, :], preferred_element_type=F32)
            if first:
                acc[g * GP : (g + 1) * GP, :] = part
            else:
                acc[g * GP : (g + 1) * GP, :] += part

    add_slots(send_ref.at[me_s], ids_ref.at[me_s], True)

    for i in range(1, S):
        ids_copy(i).wait_recv()
        a_copy(i).wait_recv()
        add_slots(recv.at[i], ids_recv.at[i], False)

    def piece(j):
        return acc[pl.ds(pl.multiple_of(j * half, 16), half), :]

    for i in range(1, D):
        zsend[i] = piece(at_dev(i)).astype(BF16)
        z_copy(i).start()
    total = piece(me_d) + rhs_ref[...]
    for i in range(1, D):
        z_copy(i).wait_recv()
        total = total + zrecv[i].astype(F32)
    red[me_d] = total.astype(BF16)
    for i in range(1, D):
        g_copy(i).start()
    for i in range(1, D):
        g_copy(i).wait_recv()

    whole = red[...].reshape(D * half, red.shape[2])

    def product(k):
        rows = schur_ref[pl.ds(pl.multiple_of(k * half, 16), half), :]
        return jnp.dot(rows, whole, preferred_element_type=F32)

    for i in range(1, S):
        psend[i] = product(at_sec(i)).astype(BF16)
        p_copy(i).start()
    total = product(me_s)
    for i in range(1, S):
        p_copy(i).wait_recv()
        total = total + precv[i].astype(F32)
    value = total.astype(BF16)
    band[me_s] = value
    zval[me_d, parity] = value
    f_copy(0).start()
    for i in range(1, D):
        w_copy(i).start()
    for i in range(1, S):
        v_copy(i).start()
    for i in range(1, D):
        w_copy(i).wait_recv()
        f_copy(i).start()
    for i in range(D):
        f_copy(i).wait_recv()

    def gather(ids, put):
        for g in range(D // G):
            hot = jnp.where(
                lax.broadcasted_iota(jnp.int32, (GP, GC), 0) == ids[8 + g : 9 + g, :GC], 1.0, 0.0
            ).astype(BF16)
            rows = zval[g * G : (g + 1) * G].reshape(GP, zval.shape[3])
            got = lax.dot_general(
                hot, rows, (((0,), (0,)), ((), ())), preferred_element_type=F32
            )
            put(g, got.astype(BF16))

    for t in range(1, S // 2):
        def put(g, got, t=t):
            gsend[t, g * GC : (g + 1) * GC, :] = got

        gather(ids_recv.at[S - 2 * t], put)
        k_copy(t).start()

    def put_own(g, got):
        picked[quarter, g * GC : (g + 1) * GC, :] = got

    gather(ids_ref.at[me_s], put_own)

    for i in range(1, S):
        v_copy(i).wait_recv()
    out_values = pltpu.make_async_copy(band, values_ref, s_o.at[0])
    out_values.start()
    for t in range(1, S // 2):
        k_copy(t).wait_recv()
    out_picked = pltpu.make_async_copy(picked, picked_ref, s_o.at[1])
    out_picked.start()
    for i in range(1, S):
        ids_copy(i).wait_send()
        a_copy(i).wait_send()
        p_copy(i).wait_send()
        v_copy(i).wait_send()
    for i in range(1, D):
        z_copy(i).wait_send()
        g_copy(i).wait_send()
        w_copy(i).wait_send()
    for i in range(D):
        f_copy(i).wait_send()
    for t in range(1, S // 2):
        k_copy(t).wait_send()
    out_values.wait()
    out_picked.wait()


def place_kernel(place_ref, picked_ref, out_ref):
    count, total = place_ref.shape[0], picked_ref.shape[0]
    hot = jnp.where(
        place_ref[...] == lax.broadcasted_iota(jnp.int32, (count, total), 1), 1.0, 0.0
    ).astype(BF16)
    out_ref[...] = jnp.dot(hot, picked_ref[...], preferred_element_type=F32).astype(BF16)


def shards(
    rhs_interior, rhs_interface, inv_blocks, coupling, interface_map, slot_counts, column_order, schur_inverse
):
    NB, B = inv_blocks.shape[:2]
    K = coupling.shape[2]
    N = rhs_interior.shape[1]
    S, D = lax.axis_size("sec"), lax.axis_size("dev")
    rows_all = schur_inverse.shape[0] * D
    NP = S * D // 2
    PR = rows_all // NP
    slots = NB * K
    C = slots // NP
    G = 16 // math.gcd(16, C)
    GC = G * C
    L = -(-GC // 128) * 128
    half = PR // 2

    live = jnp.arange(K, dtype=jnp.int32)[None, :] < slot_counts[:, None]
    pair = interface_map // PR
    mine = pair[:, :, None] == jnp.arange(NP, dtype=jnp.int32)[None, None, :]
    hot = mine.astype(BF16)
    upto = jnp.tril(jnp.ones((K, K), BF16))
    within = jnp.einsum("kl,blp->bkp", upto, hot, preferred_element_type=F32)
    before = jnp.dot(
        jnp.tril(jnp.ones((NB, NB), BF16), -1), within[:, -1, :].astype(BF16), preferred_element_type=F32
    )
    rank = jnp.sum(jnp.where(mine, within + before[:, None, :], 0.0), axis=2).astype(jnp.int32) - 1
    local = interface_map - pair * PR
    place_a = pair * C + rank
    place_c = ((pair % (S // 2)) * D + pair // (S // 2)) * C + rank
    place_c = jnp.where(live, place_c, -1).reshape(slots, 1)
    digits = jnp.stack([local // 128, local % 128]).reshape(2, slots).astype(BF16)
    digits = jnp.pad(digits, ((0, 14), (0, 0)))

    solved = jnp.einsum(
        "bij,bjn->bin", inv_blocks, rhs_interior.reshape(NB, B, N), preferred_element_type=F32
    ).astype(BF16)
    partials = jnp.einsum("bkr,brn->bkn", coupling[:, 0], solved, preferred_element_type=F32)
    partials = jnp.where(live[:, :, None], -partials, 0.0).astype(BF16).reshape(slots, N)

    step = slots // S
    full = lambda *shape: pl.BlockSpec(shape, lambda i: (0,) * len(shape))
    ordered, id_digits = pl.pallas_call(
        sort_kernel,
        grid=(S,),
        in_specs=[full(1, slots), full(16, slots), full(slots, N)],
        out_specs=[
            pl.BlockSpec((step, N), lambda i: (i, 0)),
            pl.BlockSpec((1, 16, step), lambda i: (i, 0, 0)),
        ],
        out_shape=[
            jax.ShapeDtypeStruct((slots, N), BF16),
            jax.ShapeDtypeStruct((S, 16, step), F32),
        ],
        compiler_params=pltpu.CompilerParams(vmem_limit_bytes=VMEM_LIMIT),
    )(place_a.reshape(1, slots), digits, partials)
    ids = (id_digits[:, 0] * 128.0 + id_digits[:, 1]).astype(jnp.int32).reshape(NP, C)
    ids_a = ids.reshape(S, D // 2 // G, G, C) + (jnp.arange(G, dtype=jnp.int32) * PR)[None, None, :, None]
    ids_c = ids.reshape(D // G, G, S // 2, C) + (jnp.arange(G, dtype=jnp.int32) * PR)[None, :, None, None]
    ids_a = jnp.pad(ids_a.reshape(S, D // 2 // G, GC), ((0, 0), (0, 8 - D // 2 // G), (0, L - GC)))
    ids_c = jnp.transpose(ids_c, (2, 0, 1, 3)).reshape(S // 2, D // G, GC)
    ids_c = jnp.repeat(jnp.pad(ids_c, ((0, 0), (0, 8 - D // G), (0, L - GC))), 2, axis=0)
    ids_all = jnp.concatenate([ids_a, ids_c], axis=1)

    rhs_cols = jnp.take(rhs_interface, column_order, axis=1)

    vm = pl.BlockSpec(memory_space=pltpu.VMEM)
    anyspace = pl.BlockSpec(memory_space=pl.ANY)
    dma = pltpu.SemaphoreType.DMA
    values, picked = pl.pallas_call(
        functools.partial(interface_kernel, S, D, C, PR, G),
        in_specs=[vm] * 4,
        out_specs=[anyspace] * 2,
        out_shape=[
            jax.ShapeDtypeStruct((S, half, N), BF16),
            jax.ShapeDtypeStruct((S // 2, D * C, N), BF16),
        ],
        scratch_shapes=[
            pltpu.VMEM((S, D // 2 * C, N), BF16),
            pltpu.VMEM((S, 16, L), jnp.int32),
            pltpu.VMEM((D * half, N), F32),
            pltpu.VMEM((D, half, N), BF16),
            pltpu.VMEM((D, half, N), BF16),
            pltpu.VMEM((D, half, N), BF16),
            pltpu.VMEM((S, half, N), BF16),
            pltpu.VMEM((S, half, N), BF16),
            pltpu.VMEM((S, half, N), BF16),
            pltpu.VMEM((D, 2, half, N), BF16),
            pltpu.VMEM((S // 2, D * C, N), BF16),
            pltpu.VMEM((S // 2, D * C, N), BF16),
            dma((S,)), dma((S,)), dma((S,)), dma((S,)), dma((D,)), dma((D,)), dma((D,)), dma((D,)),
            dma((S,)), dma((S,)), dma((S,)), dma((S,)), dma((D,)), dma((D,)), dma((D,)), dma((D,)),
            dma((S // 2,)), dma((S // 2,)), dma((2,)),
        ],
        compiler_params=pltpu.CompilerParams(
            collective_id=0, has_side_effects=True, vmem_limit_bytes=VMEM_LIMIT
        ),
    )(ordered.reshape(S, step, N), ids_all, rhs_cols, schur_inverse)

    interface_solution = values.reshape(S * half, N).astype(F32)
    picked = pl.pallas_call(
        place_kernel,
        grid=(S,),
        in_specs=[pl.BlockSpec((step, 1), lambda i: (i, 0)), full(slots, N)],
        out_specs=pl.BlockSpec((step, N), lambda i: (i, 0)),
        out_shape=jax.ShapeDtypeStruct((slots, N), BF16),
        compiler_params=pltpu.CompilerParams(vmem_limit_bytes=VMEM_LIMIT),
    )(place_c, picked.reshape(slots, N)).reshape(NB, K, N)

    pushed = jnp.einsum("bkr,bkn->brn", coupling[:, 1], picked, preferred_element_type=F32).astype(BF16)
    back_term = jnp.einsum("bij,bjn->bin", inv_blocks, pushed, preferred_element_type=F32)
    interior = (solved.astype(F32) - back_term).astype(BF16)
    return (interior.reshape(NB * B, N), interface_solution)


def solution(mesh):
    placed = (
        P(("sec", "dev"), None),
        P(("sec", "dev"), None),
        P(("sec", "dev"), None, None),
        P(("sec", "dev"), None, None, None),
        P(("sec", "dev"), None),
        P(("sec", "dev")),
        P(),
        P("dev", "sec"),
    )
    return jax.shard_map(
        shards,
        mesh=mesh,
        in_specs=placed,
        out_specs=(P(("sec", "dev"), None), P("dev", None)),
        check_vma=False,
    )
```

time: 384 us -> 152 us (0.40); the launches traced: 379 us -> 152 us
  waiting for transfers between devices: 243 us -> 0 us
  Pallas kernels: 0 us -> 119 us
  blocking collectives: 47.6 us -> 0 us
  other arithmetic: 26.1 us -> 7.92 us
  local copies, waits for them, and re-layouts: 22 us -> 5.11 us
  between operations: 13.8 us -> 0.78 us
  matrix products: 26.5 us -> 18.4 us
    pallas_call x0 -> x3, Pallas kernels: none -> 119 us  [the longest x1 101 us: shards(): pl.pallas_call(functools.partial(interface_kernel, S, D, C, PR, G), in_sp...]
    all_gather x1 -> x0, waiting for transfers between devices: 93.4 us -> none  [shards(): lax.all_gather(interface_solution.astype(jnp.bfloat16), 'dev', axis=0, ti...]
    reduce_scatter x1 -> x0, waiting for transfers between devices: 82.7 us -> none  [shards(): lax.psum_scatter(dense_sums, 'sec', scatter_dimension=0, tiled=True)]
    psum x1 -> x0, waiting for transfers between devices: 66.7 us -> none  [shards(): interface_solution = lax.psum(schur_part, 'sec')]
    psum x1 -> x0, blocking collectives: 47.6 us -> none  [shards(): reduced = lax.psum(section_part, 'dev')]
    scatter-add x1 -> x0, other arithmetic: 18.9 us -> none  [shards(): jnp.zeros((interface_rows, column_count), jnp.float32).at[targets]]
    gather x1 -> x0, local copies, waits for them, and re-layouts: 8.89 us -> none  [shards(): jnp.take(values, interface_map.reshape(-1), axis=0)]
    all_gather x1 -> x0, local copies, waits for them, and re-layouts: 7.91 us -> none  [shards(): lax.all_gather(interface_solution.astype(jnp.bfloat16), 'dev', axis=0, ti...]
  transfers between devices with their start and end apart: 3 -> 0, of which waited for: 3 -> 0; matrix products, arithmetic and copies ran while one was open for 1% -> 0% of each run, Pallas kernels for 0% -> 0%
where the time goes in v1:
time: 152 us
  Pallas kernels  119 us (78%)
  matrix products  18.4 us (12%)
  other arithmetic  7.92 us (5%)
  local copies, waits for them, and re-layouts  5.11 us (3%)
    pallas_call x1, Pallas kernels, shards(): pl.pallas_call(functools.partial(interface_kernel, S, D, C, PR, G), in_sp...  101 us
    pallas_call x1, Pallas kernels, shards(): pl.pallas_call(sort_kernel, grid=(S,), in_specs=[full(1, slots), full(16,...  10.1 us
    dot_general x1, matrix products, shards(): jnp.einsum('bij,bjn->bin', inv_blocks, pushed, preferred_element_type=F32)  9.76 us
    pallas_call x1, Pallas kernels, shards(): pl.pallas_call(place_kernel, grid=(S,), in_specs=[pl.BlockSpec((step, 1),...  8.26 us
    dot_general x1, matrix products, shards(): jnp.einsum('bij,bjn->bin', inv_blocks, rhs_interior.reshape(NB, B, N), pr...  5.72 us

profile of v1, /device:TPU:25, one launch (start us, length us, event | category | flops | bytes accessed | tf_op | source)
XLA Modules:
  0.0 151.6 jit_solution(7465683654250436205)
XLA Ops:
  0.6 0.7 add_select_fusion.4
  1.4 0.2 fusion.14
  1.6 0.3 slice_reduce_fusion
  1.9 0.2 fusion.37
  2.1 0.2 fusion.13
  2.2 0.8 multiply_add_fusion
  3.0 0.1 stack.10
  3.2 0.7 fusion.18.local_ref
  3.9 0.7 reshape.107.place_ref
  4.6 5.7 %convolution_convert_fusion = bf16[40,256,256]{2,1,0:T(8,128)(2,1)S(1)} fusion(bf16[40,256,256]{2,1,0:T(8,128)(2,1)} %param.10, bf16[40,256,256]{2,1,0:T(8,128)(2,1)} %bitcast.46), kind=kOutput, calls=%fused_computation.6 | convolution fusion | flops 1344798720 | bytes 15728640 | tf_op jit(solution)/shard_map/bij,bjn->bin/dot_general | solution.py:244
  10.4 2.5 %select_convert_fusion = bf16[40,256,64]{1,2,0:T(8,128)(2,1)} fusion(bf16[40,256,256]{2,1,0:T(8,128)(2,1)S(1)} %convolution_convert_fusion, bf16[40,2,64,256]{3,2,1,0:T(8,128)(2,1)S(1)} %copy-done.1, pred[40,64]{1,0:T(8,128)(4,1)S(1)} %iota_compare_fusion.5), kind=kOutput, calls=%fused_computation.7 | convolution fusion | flops 337510400 | bytes 7869440 | tf_op jit(solution)/shard_map/bkr,brn->bkn/dot_general | solution.py:247
  12.9 0.2 copy-done
  13.1 10.1 %shard_map.95 = (bf16[2560,256]{1,0:T(8,128)(2,1)}, f32[8,16,320]{2,1,0:T(8,128)}) custom-call(s32[1,2560]{1,0:T(1,128)} %reshape.107.place_ref, bf16[16,2560]{1,0:T(8,128)(2,1)} %fusion.18.local_ref, bf16[2560,256]{1,0:T(8,128)(2,1)} %bitcast.48), custom_call_target="tpu_custom_call" | custom-call | tf_op jit(solution)/shard_map/pallas_call | solution.py:252
  23.2 1.0 convert_reduce_fusion
  24.4 0.6 pad_add_fusion.ids_ref
  25.1 0.2 copy.16
  25.3 1.0 gather_fusion
  26.2 0.1 copy.17
  26.4 0.7 select_bitcast_fusion.rhs_ref
  27.2 101.1 %shard_map.96 = (bf16[8,320,256]{2,1,0:T(8,128)(2,1)}, bf16[4,640,256]{2,1,0:T(8,128)(2,1)}) custom-call(bf16[8,320,256]{2,1,0:T(8,128)(2,1)} %bitcast.49, s32[8,16,256]{2,1,0:T(8,128)} %pad_add_fusion.ids_ref, f32[320,256]{1,0:T(8,128)} %select_bitcast_fusion.rhs_ref, bf16[2560,1280]{1,0:T(8,128)(2,1)} %schur_ref.1), custom_call_target="tpu_custom_call" | custom-call | tf_op jit(solution)/shard_map/pallas_call | solution.py:279
  128.2 2.3 %reshape.126.place_ref = s32[2560,1]{1,0:T(8,128)} reshape(s32[40,64]{1,0:T(8,128)S(1)} %get-tuple-element.11) | data formatting | bytes 20480 | tf_op jit(solution)/shard_map/reshape | solution.py:240
  130.6 8.3 %shard_map.97 = bf16[2560,256]{1,0:T(8,128)(2,1)} custom-call(s32[2560,1]{1,0:T(8,128)} %reshape.126.place_ref, bf16[2560,256]{1,0:T(8,128)(2,1)} %bitcast.50), custom_call_target="tpu_custom_call" | custom-call | tf_op jit(solution)/shard_map/pallas_call | solution.py:310
  138.8 9.8 %fusion = bf16[40,256,256]{2,1,0:T(8,128)(2,1)} fusion(bf16[40,256,256]{2,1,0:T(8,128)(2,1)} %copy-done, bf16[40,256,256]{2,1,0:T(8,128)(2,1)} %param.10, bf16[40,64,256]{2,1,0:T(8,128)(2,1)} %bitcast.45, bf16[40,2,64,256]{3,2,1,0:T(8,128)(2,1)S(1)} %copy-done.1), kind=kOutput, calls=%fused_computation.2 | convolution fusion | flops 1688207360 | bytes 18350080 | tf_op jit(solution)/shard_map/bij,bjn->bin/dot_general | solution.py:320
  148.6 3.0 %bitcast_convert_fusion = f32[2560,256]{1,0:T(8,128)} fusion(bf16[8,320,256]{2,1,0:T(8,128)(2,1)} %get-tuple-element.9), kind=kLoop, calls=%fused_computation.9 | loop fusion | flops 655360 | bytes 3932160 | tf_op jit(solution)/shard_map/convert_element_type | solution.py:309
  (21 shorter events, 0.4 us)
Async XLA Ops:
  4.6 5.7 %copy-start.3 = (s32[40]{0:T(128)S(1)}, s32[40]{0:T(128)}, u32[]{:S(2)}) copy-start(s32[40]{0:T(128)} %param.13) | copy-start | bytes 484
  4.6 5.8 %copy-start.1 = (bf16[40,2,64,256]{3,2,1,0:T(8,128)(2,1)S(1)}, bf16[40,2,64,256]{3,2,1,0:T(8,128)(2,1)}, u32[]{:S(2)}) copy-start(bf16[40,2,64,256]{3,2,1,0:T(8,128)(2,1)} %param.11) | copy-start | bytes 7864324
  10.3 2.8 %copy-start = (bf16[40,256,256]{2,1,0:T(8,128)(2,1)}, bf16[40,256,256]{2,1,0:T(8,128)(2,1)S(1)}, u32[]{:S(2)}) copy-start(bf16[40,256,256]{2,1,0:T(8,128)(2,1)S(1)} %convolution_convert_fusion) | copy-start | bytes 15728644
  10.4 14.7 %copy-start.2 = (f32[320,256]{1,0:T(8,128)S(1)}, f32[320,256]{1,0:T(8,128)}, u32[]{:S(2)}) copy-start(f32[320,256]{1,0:T(8,128)} %param.9) | copy-start | bytes 983044
  13.1 12.2 %copy-start.4 = (s32[256]{0:T(256)S(1)}, s32[256]{0:T(256)}, u32[]{:S(2)}) copy-start(s32[256]{0:T(256)} %param.14) | copy-start | bytes 3076

commit v2 on v1

--- a/solution.py
+++ b/solution.py
@@ -12,6 +12,7 @@
 F32 = jnp.float32
 BF16 = jnp.bfloat16
 VMEM_LIMIT = 56 * 1024 * 1024
+PARTS = 2
 
 
 def sort_kernel(place_ref, local_ref, rows_ref, sorted_ref, ids_ref):
@@ -28,15 +29,21 @@
     S, D, C, PR, G,
     send_ref, ids_ref, rhs_ref, schur_ref,
     values_ref, picked_ref,
-    recv, ids_recv, acc, zsend, zrecv, red, psend, precv, band, zval, gsend, picked,
-    s_a, r_a, s_i, r_i, s_z, r_z, s_g, r_g, s_p, r_p, s_v, r_v, s_w, r_w, s_f, r_f, s_k, r_k, s_o,
+    recv, ids_recv, acc, zsend, zrecv, red, own, msend, mrecv, psend, precv, band, zval, gsend, picked,
+    s_i, r_i, s_a, r_a, s_z, r_z, s_g, r_g, s_m, r_m, s_p, r_p, s_v, r_v, s_u, r_u, s_w, r_w, s_f, r_f, s_k, r_k, s_o,
 ):
     me_s, me_d = lax.axis_index("sec"), lax.axis_index("dev")
     half = PR // 2
+    Q = S // 2
     GC, GP = G * C, G * PR
     parity = lax.rem(me_s, 2)
     mate = me_s + 1 - 2 * parity
     quarter = me_s // 2
+    width = rhs_ref.shape[1] // PARTS
+    parts = range(PARTS)
+
+    def cols(h):
+        return pl.ds(h * width, width)
 
     def at_sec(i):
         return lax.rem(me_s + i, S)
@@ -60,141 +67,179 @@
     def ids_copy(i):
         return copy(ids_ref.at[at_sec(i)], ids_recv.at[i], s_i.at[i], r_i.at[i], at_sec(i), me_d)
 
-    def a_copy(i):
-        return copy(send_ref.at[at_sec(i)], recv.at[i], s_a.at[i], r_a.at[i], at_sec(i), me_d)
-
-    def z_copy(i):
-        return copy(zsend.at[i], zrecv.at[i], s_z.at[i], r_z.at[i], me_s, at_dev(i))
-
-    def g_copy(i):
-        return copy(red.at[me_d], red.at[me_d], s_g.at[i], r_g.at[i], me_s, at_dev(i))
-
-    def p_copy(i):
-        return copy(psend.at[i], precv.at[i], s_p.at[i], r_p.at[i], at_sec(i), me_d)
-
-    def v_copy(i):
-        return copy(band.at[me_s], band.at[me_s], s_v.at[i], r_v.at[i], at_sec(i), me_d)
-
-    def w_copy(i):
-        return copy(band.at[me_s], zval.at[me_d, parity], s_w.at[i], r_w.at[i], me_s, at_dev(i))
-
-    def f_copy(i):
-        from_dev = lax.rem(me_d - i + D, D)
-        src = band.at[me_s] if i == 0 else zval.at[from_dev, parity]
-        return copy(src, zval.at[from_dev, parity], s_f.at[i], r_f.at[i], mate, me_d)
-
-    def k_copy(t):
-        return copy(gsend.at[t], picked.at[quarter], s_k.at[t], r_k.at[t], at_sec(2 * t), me_d)
+    def part_copy(src, dst, h, i, send, recv_sem, sec, dev):
+        return copy(src.at[:, cols(h)], dst.at[:, cols(h)], send.at[h, i], recv_sem.at[h, i], sec, dev)
+
+    def a_copy(h, i):
+        return part_copy(send_ref.at[at_sec(i)], recv.at[i], h, i, s_a, r_a, at_sec(i), me_d)
+
+    def z_copy(h, i):
+        return part_copy(zsend.at[i], zrecv.at[i], h, i, s_z, r_z, me_s, at_dev(i))
+
+    def g_copy(h, i):
+        return part_copy(red.at[me_d], red.at[me_d], h, i, s_g, r_g, me_s, at_dev(i))
+
+    def m_copy(h, t):
+        return part_copy(msend.at[t], mrecv.at[t], h, t, s_m, r_m, mate, me_d)
+
+    def p_copy(h, t):
+        return part_copy(psend.at[t], precv.at[t], h, t, s_p, r_p, at_sec(2 * t), me_d)
+
+    def v_copy(h, t):
+        return part_copy(band.at[me_s], band.at[me_s], h, t, s_v, r_v, at_sec(2 * t), me_d)
+
+    def u_copy(h, t):
+        k = lax.rem(me_s - 2 * t + S, S)
+        return part_copy(band.at[k], band.at[k], h, t, s_u, r_u, mate, me_d)
+
+    def w_copy(h, i):
+        return part_copy(band.at[me_s], zval.at[me_d, parity], h, i, s_w, r_w, me_s, at_dev(i))
+
+    def f_copy(h, i):
+        k = lax.rem(me_d - i + D, D)
+        src = band.at[me_s] if i == 0 else zval.at[k, parity]
+        return part_copy(src, zval.at[k, parity], h, i, s_f, r_f, mate, me_d)
+
+    def k_copy(h, t):
+        return part_copy(gsend.at[t], picked.at[quarter], h, t, s_k, r_k, at_sec(2 * t), me_d)
 
     for i in range(1, S):
         ids_copy(i).start()
-        a_copy(i).start()
-
-    def add_slots(rows, ids, first):
+    for h in parts:
+        for i in range(1, S):
+            a_copy(h, i).start()
+
+    def add_slots(rows, ids, h, first):
         for g in range(D // 2 // G):
             hot = jnp.where(
                 lax.broadcasted_iota(jnp.int32, (GP, GC), 0) == ids[g : g + 1, :GC], 1.0, 0.0
             ).astype(BF16)
-            part = jnp.dot(hot, rows[g * GC : (g + 1) * GC, :], preferred_element_type=F32)
+            part = jnp.dot(hot, rows[g * GC : (g + 1) * GC, cols(h)], preferred_element_type=F32)
             if first:
-                acc[g * GP : (g + 1) * GP, :] = part
+                acc[g * GP : (g + 1) * GP, cols(h)] = part
             else:
-                acc[g * GP : (g + 1) * GP, :] += part
-
-    add_slots(send_ref.at[me_s], ids_ref.at[me_s], True)
-
-    for i in range(1, S):
-        ids_copy(i).wait_recv()
-        a_copy(i).wait_recv()
-        add_slots(recv.at[i], ids_recv.at[i], False)
-
-    def piece(j):
-        return acc[pl.ds(pl.multiple_of(j * half, 16), half), :]
-
-    for i in range(1, D):
-        zsend[i] = piece(at_dev(i)).astype(BF16)
-        z_copy(i).start()
-    total = piece(me_d) + rhs_ref[...]
-    for i in range(1, D):
-        z_copy(i).wait_recv()
-        total = total + zrecv[i].astype(F32)
-    red[me_d] = total.astype(BF16)
-    for i in range(1, D):
-        g_copy(i).start()
-    for i in range(1, D):
-        g_copy(i).wait_recv()
-
-    whole = red[...].reshape(D * half, red.shape[2])
-
-    def product(k):
-        rows = schur_ref[pl.ds(pl.multiple_of(k * half, 16), half), :]
-        return jnp.dot(rows, whole, preferred_element_type=F32)
-
-    for i in range(1, S):
-        psend[i] = product(at_sec(i)).astype(BF16)
-        p_copy(i).start()
-    total = product(me_s)
-    for i in range(1, S):
-        p_copy(i).wait_recv()
-        total = total + precv[i].astype(F32)
-    value = total.astype(BF16)
-    band[me_s] = value
-    zval[me_d, parity] = value
-    f_copy(0).start()
-    for i in range(1, D):
-        w_copy(i).start()
-    for i in range(1, S):
-        v_copy(i).start()
-    for i in range(1, D):
-        w_copy(i).wait_recv()
-        f_copy(i).start()
-    for i in range(D):
-        f_copy(i).wait_recv()
-
-    def gather(ids, put):
+                acc[g * GP : (g + 1) * GP, cols(h)] += part
+
+    def piece(j, h):
+        return acc[pl.ds(pl.multiple_of(j * half, 16), half), cols(h)]
+
+    for h in parts:
+        add_slots(send_ref.at[me_s], ids_ref.at[me_s], h, True)
+    for h in parts:
+        for i in range(1, S):
+            if h == 0:
+                ids_copy(i).wait_recv()
+            a_copy(h, i).wait_recv()
+            add_slots(recv.at[i], ids_recv.at[i], h, False)
+        for i in range(1, D):
+            zsend[i, :, cols(h)] = piece(at_dev(i), h).astype(BF16)
+            z_copy(h, i).start()
+    for h in parts:
+        total = piece(me_d, h) + rhs_ref[:, cols(h)]
+        for i in range(1, D):
+            z_copy(h, i).wait_recv()
+            total = total + zrecv[i, :, cols(h)].astype(F32)
+        red[me_d, :, cols(h)] = total.astype(BF16)
+        for i in range(1, D):
+            g_copy(h, i).start()
+
+    for h in parts:
+        for i in range(1, D):
+            g_copy(h, i).wait_recv()
+        whole = red[:, :, cols(h)].reshape(D * half, width)
+
+        def product(k):
+            rows = schur_ref[pl.ds(pl.multiple_of(k * half, 16), half), :]
+            return jnp.dot(rows, whole, preferred_element_type=F32)
+
+        order = [*range(1, Q), 0]
+        for t in order:
+            msend[t, :, cols(h)] = product(lax.rem(mate + 2 * t, S)).astype(BF16)
+            m_copy(h, t).start()
+        for t in order:
+            total = product(at_sec(2 * t))
+            m_copy(h, t).wait_recv()
+            total = total + mrecv[t, :, cols(h)].astype(F32)
+            if t:
+                psend[t, :, cols(h)] = total.astype(BF16)
+                p_copy(h, t).start()
+            else:
+                own[:, cols(h)] = total
+    for h in parts:
+        total = own[:, cols(h)]
+        for t in range(1, Q):
+            p_copy(h, t).wait_recv()
+            total = total + precv[t, :, cols(h)].astype(F32)
+        value = total.astype(BF16)
+        band[me_s, :, cols(h)] = value
+        zval[me_d, parity, :, cols(h)] = value
+        f_copy(h, 0).start()
+        for i in range(1, D):
+            w_copy(h, i).start()
+        for t in range(1, Q):
+            v_copy(h, t).start()
+
+    def gather(ids, h, put):
         for g in range(D // G):
             hot = jnp.where(
                 lax.broadcasted_iota(jnp.int32, (GP, GC), 0) == ids[8 + g : 9 + g, :GC], 1.0, 0.0
             ).astype(BF16)
-            rows = zval[g * G : (g + 1) * G].reshape(GP, zval.shape[3])
+            rows = zval[g * G : (g + 1) * G, :, :, cols(h)].reshape(GP, width)
             got = lax.dot_general(
                 hot, rows, (((0,), (0,)), ((), ())), preferred_element_type=F32
             )
             put(g, got.astype(BF16))
 
-    for t in range(1, S // 2):
-        def put(g, got, t=t):
-            gsend[t, g * GC : (g + 1) * GC, :] = got
-
-        gather(ids_recv.at[S - 2 * t], put)
-        k_copy(t).start()
-
-    def put_own(g, got):
-        picked[quarter, g * GC : (g + 1) * GC, :] = got
-
-    gather(ids_ref.at[me_s], put_own)
-
-    for i in range(1, S):
-        v_copy(i).wait_recv()
+    for h in parts:
+        for i in range(1, D):
+            w_copy(h, i).wait_recv()
+            f_copy(h, i).start()
+        for i in range(D):
+            f_copy(h, i).wait_recv()
+        for t in range(1, Q):
+            def put(g, got):
+                gsend[t, g * GC : (g + 1) * GC, cols(h)] = got
+
+            gather(ids_recv.at[S - 2 * t], h, put)
+            k_copy(h, t).start()
+        for t in range(1, Q):
+            v_copy(h, t).wait_recv()
+            u_copy(h, t).start()
+
+    for h in parts:
+        def put_own(g, got):
+            picked[quarter, g * GC : (g + 1) * GC, cols(h)] = got
+
+        gather(ids_ref.at[me_s], h, put_own)
+        band[mate, :, cols(h)] = zval[me_d, 1 - parity, :, cols(h)]
+    for h in parts:
+        for t in range(1, Q):
+            u_copy(h, t).wait_recv()
     out_values = pltpu.make_async_copy(band, values_ref, s_o.at[0])
     out_values.start()
-    for t in range(1, S // 2):
-        k_copy(t).wait_recv()
+    for h in parts:
+        for t in range(1, Q):
+            k_copy(h, t).wait_recv()
     out_picked = pltpu.make_async_copy(picked, picked_ref, s_o.at[1])
     out_picked.start()
     for i in range(1, S):
         ids_copy(i).wait_send()
-        a_copy(i).wait_send()
-        p_copy(i).wait_send()
-        v_copy(i).wait_send()
-    for i in range(1, D):
-        z_copy(i).wait_send()
-        g_copy(i).wait_send()
-        w_copy(i).wait_send()
-    for i in range(D):
-        f_copy(i).wait_send()
-    for t in range(1, S // 2):
-        k_copy(t).wait_send()
+    for h in parts:
+        for i in range(1, S):
+            a_copy(h, i).wait_send()
+        for i in range(1, D):
+            z_copy(h, i).wait_send()
+            g_copy(h, i).wait_send()
+            w_copy(h, i).wait_send()
+        for i in range(D):
+            f_copy(h, i).wait_send()
+        for t in range(Q):
+            m_copy(h, t).wait_send()
+        for t in range(1, Q):
+            p_copy(h, t).wait_send()
+            v_copy(h, t).wait_send()
+            u_copy(h, t).wait_send()
+            k_copy(h, t).wait_send()
     out_values.wait()
     out_picked.wait()
 
@@ -291,15 +336,19 @@
             pltpu.VMEM((D, half, N), BF16),
             pltpu.VMEM((D, half, N), BF16),
             pltpu.VMEM((D, half, N), BF16),
-            pltpu.VMEM((S, half, N), BF16),
-            pltpu.VMEM((S, half, N), BF16),
+            pltpu.VMEM((half, N), F32),
+            *[pltpu.VMEM((S // 2, half, N), BF16)] * 4,
             pltpu.VMEM((S, half, N), BF16),
             pltpu.VMEM((D, 2, half, N), BF16),
             pltpu.VMEM((S // 2, D * C, N), BF16),
             pltpu.VMEM((S // 2, D * C, N), BF16),
-            dma((S,)), dma((S,)), dma((S,)), dma((S,)), dma((D,)), dma((D,)), dma((D,)), dma((D,)),
-            dma((S,)), dma((S,)), dma((S,)), dma((S,)), dma((D,)), dma((D,)), dma((D,)), dma((D,)),
-            dma((S // 2,)), dma((S // 2,)), dma((2,)),
+            dma((S,)), dma((S,)),
+            *[dma((PARTS, S))] * 2,
+            *[dma((PARTS, D))] * 4,
+            *[dma((PARTS, S // 2))] * 8,
+            *[dma((PARTS, D))] * 4,
+            *[dma((PARTS, S // 2))] * 2,
+            dma((2,)),
         ],
         compiler_params=pltpu.CompilerParams(
             collective_id=0, has_side_effects=True, vmem_limit_bytes=VMEM_LIMIT

time: 152 us -> 137 us (0.901)
  Pallas kernels: 119 us -> 105 us
    pallas_call x1, Pallas kernels: 101 us -> 86.4 us  [shards(): pl.pallas_call(functools.partial(interface_kernel, S, D, C, PR, G), in_sp...]
where the time goes in v2:
time: 137 us
  Pallas kernels  105 us (77%)
  matrix products  18.4 us (13%)
  other arithmetic  7.92 us (6%)
  local copies, waits for them, and re-layouts  5.11 us (4%)
    pallas_call x1, Pallas kernels, shards(): pl.pallas_call(functools.partial(interface_kernel, S, D, C, PR, G), in_sp...  86.4 us
    pallas_call x1, Pallas kernels, shards(): pl.pallas_call(sort_kernel, grid=(S,), in_specs=[full(1, slots), full(16,...  10.1 us
    dot_general x1, matrix products, shards(): jnp.einsum('bij,bjn->bin', inv_blocks, pushed, preferred_element_type=F32)  9.77 us
    pallas_call x1, Pallas kernels, shards(): pl.pallas_call(place_kernel, grid=(S,), in_specs=[pl.BlockSpec((step, 1),...  8.26 us
    dot_general x1, matrix products, shards(): jnp.einsum('bij,bjn->bin', inv_blocks, rhs_interior.reshape(NB, B, N), pr...  5.72 us
    convert_element_type x1, other arithmetic, shards(): interface_solution = values.reshape(S * half, N).astype(F32)  3.01 us

profile of v2, /device:TPU:25, one launch (start us, length us, event | category | flops | bytes accessed | tf_op | source)
XLA Modules:
  0.0 136.9 jit_solution(3917092602825721966)
XLA Ops:
  0.6 0.7 add_select_fusion.4
  1.4 0.2 fusion.14
  1.6 0.3 slice_reduce_fusion
  1.9 0.2 fusion.37
  2.1 0.2 fusion.13
  2.2 0.8 multiply_add_fusion
  3.0 0.1 stack.10
  3.2 0.7 fusion.18.local_ref
  3.9 0.7 reshape.107.place_ref
  4.6 5.7 %convolution_convert_fusion = bf16[40,256,256]{2,1,0:T(8,128)(2,1)S(1)} fusion(bf16[40,256,256]{2,1,0:T(8,128)(2,1)} %param.10, bf16[40,256,256]{2,1,0:T(8,128)(2,1)} %bitcast.46), kind=kOutput, calls=%fused_computation.6 | convolution fusion | flops 1344798720 | bytes 15728640 | tf_op jit(solution)/shard_map/bij,bjn->bin/dot_general | solution.py:289
  10.4 2.5 %select_convert_fusion = bf16[40,256,64]{1,2,0:T(8,128)(2,1)} fusion(bf16[40,256,256]{2,1,0:T(8,128)(2,1)S(1)} %convolution_convert_fusion, bf16[40,2,64,256]{3,2,1,0:T(8,128)(2,1)S(1)} %copy-done.1, pred[40,64]{1,0:T(8,128)(4,1)S(1)} %iota_compare_fusion.5), kind=kOutput, calls=%fused_computation.7 | convolution fusion | flops 337510400 | bytes 7869440 | tf_op jit(solution)/shard_map/bkr,brn->bkn/dot_general | solution.py:292
  12.9 0.2 copy-done
  13.1 10.1 %shard_map.95 = (bf16[2560,256]{1,0:T(8,128)(2,1)}, f32[8,16,320]{2,1,0:T(8,128)}) custom-call(s32[1,2560]{1,0:T(1,128)} %reshape.107.place_ref, bf16[16,2560]{1,0:T(8,128)(2,1)} %fusion.18.local_ref, bf16[2560,256]{1,0:T(8,128)(2,1)} %bitcast.48), custom_call_target="tpu_custom_call" | custom-call | tf_op jit(solution)/shard_map/pallas_call | solution.py:297
  23.2 1.0 convert_reduce_fusion
  24.4 0.6 pad_add_fusion.ids_ref
  25.1 0.2 copy.16
  25.3 1.0 gather_fusion
  26.2 0.1 copy.17
  26.4 0.7 select_bitcast_fusion.rhs_ref
  27.2 86.4 %shard_map.96 = (bf16[8,320,256]{2,1,0:T(8,128)(2,1)}, bf16[4,640,256]{2,1,0:T(8,128)(2,1)}) custom-call(bf16[8,320,256]{2,1,0:T(8,128)(2,1)} %bitcast.49, s32[8,16,256]{2,1,0:T(8,128)} %pad_add_fusion.ids_ref, f32[320,256]{1,0:T(8,128)} %select_bitcast_fusion.rhs_ref, bf16[2560,1280]{1,0:T(8,128)(2,1)} %schur_ref.1), custom_call_target="tpu_custom_call" | custom-call | tf_op jit(solution)/shard_map/pallas_call | solution.py:324
  113.5 2.3 %reshape.126.place_ref = s32[2560,1]{1,0:T(8,128)} reshape(s32[40,64]{1,0:T(8,128)S(1)} %get-tuple-element.11) | data formatting | bytes 20480 | tf_op jit(solution)/shard_map/reshape | solution.py:285
  115.9 8.3 %shard_map.97 = bf16[2560,256]{1,0:T(8,128)(2,1)} custom-call(s32[2560,1]{1,0:T(8,128)} %reshape.126.place_ref, bf16[2560,256]{1,0:T(8,128)(2,1)} %bitcast.50), custom_call_target="tpu_custom_call" | custom-call | tf_op jit(solution)/shard_map/pallas_call | solution.py:359
  124.1 9.8 %fusion = bf16[40,256,256]{2,1,0:T(8,128)(2,1)} fusion(bf16[40,256,256]{2,1,0:T(8,128)(2,1)} %copy-done, bf16[40,256,256]{2,1,0:T(8,128)(2,1)} %param.10, bf16[40,64,256]{2,1,0:T(8,128)(2,1)} %bitcast.45, bf16[40,2,64,256]{3,2,1,0:T(8,128)(2,1)S(1)} %copy-done.1), kind=kOutput, calls=%fused_computation.2 | convolution fusion | flops 1688207360 | bytes 18350080 | tf_op jit(solution)/shard_map/bij,bjn->bin/dot_general | solution.py:369
  133.9 3.0 %bitcast_convert_fusion = f32[2560,256]{1,0:T(8,128)} fusion(bf16[8,320,256]{2,1,0:T(8,128)(2,1)} %get-tuple-element.9), kind=kLoop, calls=%fused_computation.9 | loop fusion | flops 655360 | bytes 3932160 | tf_op jit(solution)/shard_map/convert_element_type | solution.py:358
  (21 shorter events, 0.4 us)
Async XLA Ops:
  4.6 5.7 %copy-start.3 = (s32[40]{0:T(128)S(1)}, s32[40]{0:T(128)}, u32[]{:S(2)}) copy-start(s32[40]{0:T(128)} %param.13) | copy-start | bytes 484
  4.6 5.8 %copy-start.1 = (bf16[40,2,64,256]{3,2,1,0:T(8,128)(2,1)S(1)}, bf16[40,2,64,256]{3,2,1,0:T(8,128)(2,1)}, u32[]{:S(2)}) copy-start(bf16[40,2,64,256]{3,2,1,0:T(8,128)(2,1)} %param.11) | copy-start | bytes 7864324
  10.3 2.8 %copy-start = (bf16[40,256,256]{2,1,0:T(8,128)(2,1)}, bf16[40,256,256]{2,1,0:T(8,128)(2,1)S(1)}, u32[]{:S(2)}) copy-start(bf16[40,256,256]{2,1,0:T(8,128)(2,1)S(1)} %convolution_convert_fusion) | copy-start | bytes 15728644
  10.4 14.7 %copy-start.2 = (f32[320,256]{1,0:T(8,128)S(1)}, f32[320,256]{1,0:T(8,128)}, u32[]{:S(2)}) copy-start(f32[320,256]{1,0:T(8,128)} %param.9) | copy-start | bytes 983044
  13.1 12.2 %copy-start.4 = (s32[256]{0:T(256)S(1)}, s32[256]{0:T(256)}, u32[]{:S(2)}) copy-start(s32[256]{0:T(256)} %param.14) | copy-start | bytes 3076

commit v3 on v2

--- a/solution.py
+++ b/solution.py
@@ -29,7 +29,7 @@
     S, D, C, PR, G,
     send_ref, ids_ref, rhs_ref, schur_ref,
     values_ref, picked_ref,
-    recv, ids_recv, acc, zsend, zrecv, red, own, msend, mrecv, psend, precv, band, zval, gsend, picked,
+    schur, recv, ids_recv, acc, zsend, zrecv, red, own, msend, mrecv, psend, precv, band, zval, gsend, picked,
     s_i, r_i, s_a, r_a, s_z, r_z, s_g, r_g, s_m, r_m, s_p, r_p, s_v, r_v, s_u, r_u, s_w, r_w, s_f, r_f, s_k, r_k, s_o,
 ):
     me_s, me_d = lax.axis_index("sec"), lax.axis_index("dev")
@@ -105,6 +105,8 @@
 
     for i in range(1, S):
         ids_copy(i).start()
+    load = pltpu.make_async_copy(schur_ref, schur, s_o.at[2])
+    load.start()
     for h in parts:
         for i in range(1, S):
             a_copy(h, i).start()
@@ -143,13 +145,15 @@
         for i in range(1, D):
             g_copy(h, i).start()
 
+    load.wait()
+
     for h in parts:
         for i in range(1, D):
             g_copy(h, i).wait_recv()
         whole = red[:, :, cols(h)].reshape(D * half, width)
 
         def product(k):
-            rows = schur_ref[pl.ds(pl.multiple_of(k * half, 16), half), :]
+            rows = schur[pl.ds(pl.multiple_of(k * half, 16), half), :]
             return jnp.dot(rows, whole, preferred_element_type=F32)
 
         order = [*range(1, Q), 0]
@@ -244,12 +248,20 @@
     out_picked.wait()
 
 
-def place_kernel(place_ref, picked_ref, out_ref):
-    count, total = place_ref.shape[0], picked_ref.shape[0]
+def back_kernel(place_ref, picked_ref, coupling_ref, inv_ref, solved_ref, out_ref):
+    blocks, K = coupling_ref.shape[0], coupling_ref.shape[1]
+    count, total = blocks * K, picked_ref.shape[0]
+    place = jnp.transpose(jnp.broadcast_to(place_ref[0], (8, count)))[:, :1].astype(jnp.int32)
     hot = jnp.where(
-        place_ref[...] == lax.broadcasted_iota(jnp.int32, (count, total), 1), 1.0, 0.0
+        place == lax.broadcasted_iota(jnp.int32, (count, total), 1), 1.0, 0.0
     ).astype(BF16)
-    out_ref[...] = jnp.dot(hot, picked_ref[...], preferred_element_type=F32).astype(BF16)
+    got = jnp.dot(hot, picked_ref[...], preferred_element_type=F32).astype(BF16)
+    for b in range(blocks):
+        pushed = lax.dot_general(
+            coupling_ref[b], got[b * K : (b + 1) * K], (((0,), (0,)), ((), ())), preferred_element_type=F32
+        ).astype(BF16)
+        back = jnp.dot(inv_ref[b], pushed, preferred_element_type=F32)
+        out_ref[b] = (solved_ref[b].astype(F32) - back).astype(BF16)
 
 
 def shards(
@@ -282,7 +294,7 @@
     local = interface_map - pair * PR
     place_a = pair * C + rank
     place_c = ((pair % (S // 2)) * D + pair // (S // 2)) * C + rank
-    place_c = jnp.where(live, place_c, -1).reshape(slots, 1)
+    place_c = jnp.where(live, place_c, -1).astype(F32)
     digits = jnp.stack([local // 128, local % 128]).reshape(2, slots).astype(BF16)
     digits = jnp.pad(digits, ((0, 14), (0, 0)))
 
@@ -323,13 +335,14 @@
     dma = pltpu.SemaphoreType.DMA
     values, picked = pl.pallas_call(
         functools.partial(interface_kernel, S, D, C, PR, G),
-        in_specs=[vm] * 4,
+        in_specs=[vm] * 3 + [anyspace],
         out_specs=[anyspace] * 2,
         out_shape=[
             jax.ShapeDtypeStruct((S, half, N), BF16),
             jax.ShapeDtypeStruct((S // 2, D * C, N), BF16),
         ],
         scratch_shapes=[
+            pltpu.VMEM(schur_inverse.shape, BF16),
             pltpu.VMEM((S, D // 2 * C, N), BF16),
             pltpu.VMEM((S, 16, L), jnp.int32),
             pltpu.VMEM((D * half, N), F32),
@@ -348,7 +361,7 @@
             *[dma((PARTS, S // 2))] * 8,
             *[dma((PARTS, D))] * 4,
             *[dma((PARTS, S // 2))] * 2,
-            dma((2,)),
+            dma((3,)),
         ],
         compiler_params=pltpu.CompilerParams(
             collective_id=0, has_side_effects=True, vmem_limit_bytes=VMEM_LIMIT
@@ -356,18 +369,21 @@
     )(ordered.reshape(S, step, N), ids_all, rhs_cols, schur_inverse)
 
     interface_solution = values.reshape(S * half, N).astype(F32)
-    picked = pl.pallas_call(
-        place_kernel,
-        grid=(S,),
-        in_specs=[pl.BlockSpec((step, 1), lambda i: (i, 0)), full(slots, N)],
-        out_specs=pl.BlockSpec((step, N), lambda i: (i, 0)),
-        out_shape=jax.ShapeDtypeStruct((slots, N), BF16),
+    group = math.gcd(NB, 4)
+    interior = pl.pallas_call(
+        back_kernel,
+        grid=(NB // group,),
+        in_specs=[
+            pl.BlockSpec((1, 1, group * K), lambda i: (i, 0, 0)),
+            full(slots, N),
+            pl.BlockSpec((group, None, K, B), lambda i: (i, 1, 0, 0)),
+            pl.BlockSpec((group, B, B), lambda i: (i, 0, 0)),
+            pl.BlockSpec((group, B, N), lambda i: (i, 0, 0)),
+        ],
+        out_specs=pl.BlockSpec((group, B, N), lambda i: (i, 0, 0)),
+        out_shape=jax.ShapeDtypeStruct((NB, B, N), BF16),
         compiler_params=pltpu.CompilerParams(vmem_limit_bytes=VMEM_LIMIT),
-    )(place_c, picked.reshape(slots, N)).reshape(NB, K, N)
-
-    pushed = jnp.einsum("bkr,bkn->brn", coupling[:, 1], picked, preferred_element_type=F32).astype(BF16)
-    back_term = jnp.einsum("bij,bjn->bin", inv_blocks, pushed, preferred_element_type=F32)
-    interior = (solved.astype(F32) - back_term).astype(BF16)
+    )(place_c.reshape(NB // group, 1, group * K), picked.reshape(slots, N), coupling, inv_blocks, solved)
     return (interior.reshape(NB * B, N), interface_solution)
 
 

time: 137 us -> 141 us (1.029)
  Pallas kernels: 105 us -> 118 us
  matrix products: 18.4 us -> 8.62 us
    pallas_call x1, Pallas kernels: 8.26 us -> 23.3 us  [shards(): pl.pallas_call(back_kernel, grid=(NB // group,), in_specs=[pl.BlockSpec((...]
    dot_general x1 -> x0, matrix products: 9.77 us -> none  [shards(): jnp.einsum('bij,bjn->bin', inv_blocks, pushed, preferred_element_type=F32)]
    pallas_call x1, Pallas kernels: 86.4 us -> 84.4 us  [shards(): pl.pallas_call(functools.partial(interface_kernel, S, D, C, PR, G), in_sp...]
    reshape x1, local copies, waits for them, and re-layouts: 2.34 us -> 0.68 us  [shards(): place_c.reshape(NB // group, 1, group * K)]
where the time goes in v3:
time: 141 us; the launch traced here: 140 us
  Pallas kernels  118 us (84%)
  other arithmetic  8.73 us (6%)
  matrix products  8.62 us (6%)
  local copies, waits for them, and re-layouts  4.52 us (3%)
    pallas_call x1, Pallas kernels, shards(): pl.pallas_call(functools.partial(interface_kernel, S, D, C, PR, G), in_sp...  84.4 us
    pallas_call x1, Pallas kernels, shards(): pl.pallas_call(back_kernel, grid=(NB // group,), in_specs=[pl.BlockSpec((...  23.3 us
    pallas_call x1, Pallas kernels, shards(): pl.pallas_call(sort_kernel, grid=(S,), in_specs=[full(1, slots), full(16,...  10.1 us
    dot_general x1, matrix products, shards(): jnp.einsum('bij,bjn->bin', inv_blocks, rhs_interior.reshape(NB, B, N), pr...  5.72 us

profile of v3, /device:TPU:25, one launch (start us, length us, event | category | flops | bytes accessed | tf_op | source)
XLA Modules:
  0.0 140.4 jit_solution(17115129908457553326)
XLA Ops:
  0.6 0.7 compare_and_fusion
  1.3 0.7 compare_select_fusion
  2.0 0.7 iota_compare_fusion.5
  2.7 0.7 add_select_fusion.4
  3.5 0.2 fusion.3
  3.7 0.3 slice_reduce_fusion
  4.0 0.2 fusion.27
  4.2 0.2 fusion.2
  4.3 0.8 multiply_add_fusion
  5.2 0.7 reshape.103.place_ref
  5.8 0.7 reshape.102.place_ref
  6.7 0.7 fusion.7.local_ref
  7.3 1.1 copy.16
  8.5 1.0 gather_fusion
  9.6 0.8 select_bitcast_fusion.rhs_ref
  10.4 5.7 %convolution_convert_fusion.solved_ref = bf16[40,256,256]{2,1,0:T(8,128)(2,1)S(1)} fusion(bf16[40,256,256]{2,1,0:T(8,128)(2,1)} %inv_ref.1, bf16[40,256,256]{2,1,0:T(8,128)(2,1)} %bitcast.34), kind=kOutput, calls=%fused_computation.1 | convolution fusion | flops 1344798720 | bytes 15728640 | tf_op jit(solution)/shard_map/bij,bjn->bin/dot_general | solution.py:301
  16.1 2.5 %select_convert_fusion = bf16[40,256,64]{1,2,0:T(8,128)(2,1)} fusion(bf16[40,256,256]{2,1,0:T(8,128)(2,1)S(1)} %convolution_convert_fusion.solved_ref, bf16[40,2,64,256]{3,2,1,0:T(8,128)(2,1)S(1)} %copy-done.1, pred[40,64]{1,0:T(8,128)(4,1)S(1)} %iota_compare_fusion.5), kind=kOutput, calls=%fused_computation.2 | convolution fusion | flops 337510400 | bytes 7869440 | tf_op jit(solution)/shard_map/bkr,brn->bkn/dot_general | solution.py:304
  18.6 0.3 copy-done
  18.9 10.1 %shard_map.95 = (bf16[2560,256]{1,0:T(8,128)(2,1)}, f32[8,16,320]{2,1,0:T(8,128)}) custom-call(s32[1,2560]{1,0:T(1,128)} %reshape.103.place_ref, bf16[16,2560]{1,0:T(8,128)(2,1)} %fusion.7.local_ref, bf16[2560,256]{1,0:T(8,128)(2,1)} %bitcast.36), custom_call_target="tpu_custom_call" | custom-call | tf_op jit(solution)/shard_map/pallas_call | solution.py:309
  29.0 1.0 convert_reduce_fusion
  30.3 0.7 pad_add_fusion.ids_ref
  30.9 84.4 %shard_map.96 = (bf16[8,320,256]{2,1,0:T(8,128)(2,1)}, bf16[4,640,256]{2,1,0:T(8,128)(2,1)}) custom-call(bf16[8,320,256]{2,1,0:T(8,128)(2,1)} %bitcast.38, s32[8,16,256]{2,1,0:T(8,128)} %pad_add_fusion.ids_ref, f32[320,256]{1,0:T(8,128)} %select_bitcast_fusion.rhs_ref, bf16[2560,1280]{1,0:T(8,128)(2,1)} %schur_ref.1), custom_call_target="tpu_custom_call" | custom-call | tf_op jit(solution)/shard_map/pallas_call | solution.py:336
  115.3 23.3 %shard_map.97 = bf16[40,256,256]{2,1,0:T(8,128)(2,1)} custom-call(f32[10,1,256]{2,1,0:T(1,128)} %reshape.102.place_ref, bf16[2560,256]{1,0:T(8,128)(2,1)} %bitcast.37, bf16[40,2,64,256]{3,2,1,0:T(8,128)(2,1)} %coupling_ref.1, bf16[40,256,256]{2,1,0:T(8,128)(2,1)} %inv_ref.1, bf16[40,256,256]{2,1,0:T(8,128)(2,1)} %copy-done), custom_call_target="tpu_custom_call" | custom-call | tf_op jit(solution)/shard_map/pallas_call | solution.py:373
  138.6 1.8 %bitcast_convert_fusion = f32[2560,256]{1,0:T(8,128)} fusion(bf16[8,320,256]{2,1,0:T(8,128)(2,1)S(1)} %copy-done.2), kind=kLoop, calls=%fused_computation.4 | loop fusion | flops 655360 | bytes 3932160 | tf_op jit(solution)/shard_map/convert_element_type | solution.py:371
  (16 shorter events, 0.5 us)
Async XLA Ops:
  10.4 5.7 %copy-start.1 = (bf16[40,2,64,256]{3,2,1,0:T(8,128)(2,1)S(1)}, bf16[40,2,64,256]{3,2,1,0:T(8,128)(2,1)}, u32[]{:S(2)}) copy-start(bf16[40,2,64,256]{3,2,1,0:T(8,128)(2,1)} %coupling_ref.1) | copy-start | bytes 7864324
  16.1 2.8 %copy-start = (bf16[40,256,256]{2,1,0:T(8,128)(2,1)}, bf16[40,256,256]{2,1,0:T(8,128)(2,1)S(1)}, u32[]{:S(2)}) copy-start(bf16[40,256,256]{2,1,0:T(8,128)(2,1)S(1)} %convolution_convert_fusion.solved_ref) | copy-start | bytes 15728644
  115.3 23.3 %copy-start.2 = (bf16[8,320,256]{2,1,0:T(8,128)(2,1)S(1)}, bf16[8,320,256]{2,1,0:T(8,128)(2,1)}, u32[]{:S(2)}) copy-start(bf16[8,320,256]{2,1,0:T(8,128)(2,1)} %get-tuple-element.9) | copy-start | bytes 3932164
